TPU v7x, 32 devices: a whole 2x2x4 slice. The times are simulated.
32 devices in a mesh: dp: 8 (over y, x, core), pipe: 4 (over z).
Axes of the slice: x: 2, y: 2, z: 4, core: 2. Of those that a mesh axis runs over, the one named last changes fastest.
Arguments:
- hidden: bfloat16 [2048, 2048], P('dp'), may hold values from -6 to 6
- gain: float32 [2048], replicated, may hold values from 0.25 to 1.75
- w_value: bfloat16 [4, 2048, 2048], P('pipe', 'dp'), may hold values from -0.125 to 0.125
- d_value: bfloat16 [4, 2048, 2048], P('pipe', 'dp'), may hold values from -3 to 3
Outputs:
- grad_hidden: bfloat16 [2048, 2048], P('dp')
- grad_gain: float32 [2048], P('dp')
- grad_value: float32 [4, 2048, 2048], P('pipe', 'dp')
All inputs are finite; a program needn't handle non-finite values.
Results may differ from a plain program's by a relative error of at most 0.0029.
Values may be sent and summed in bfloat16 or wider, within the bound.
A program may use at most 64 MiB of HBM per device.

v0:
```python
import jax
import jax.numpy as jnp
from jax import lax
from jax.sharding import PartitionSpec as P

epsilon = 1e-06


def norm_backward(grad_rows, normed_rows, scale_rows, gain):
    scaled = gain * grad_rows
    result = (
        scaled - normed_rows * jnp.mean(scaled * normed_rows, axis=-1, keepdims=True)
    ) / scale_rows
    return (result.astype(jnp.bfloat16), jnp.sum(grad_rows * normed_rows, axis=0))


def weight_term(encoded, operand):
    return lax.dot_general(
        encoded, operand, (((0,), (0,)), ((), ())), preferred_element_type=jnp.float32
    )


def local(hidden, gain, w_value, d_value):
    hidden_f = hidden.astype(jnp.float32)
    row_scale = jnp.sqrt(jnp.mean(hidden_f * hidden_f, axis=-1, keepdims=True) + epsilon)
    normed = hidden_f / row_scale
    encoded = (normed * gain).astype(jnp.bfloat16)
    cotangent = d_value[0]
    projection = w_value[0]
    average = 1.0 / lax.axis_size("dp")
    partial_value = lax.dot_general(
        cotangent,
        lax.all_gather(projection, "dp", axis=0, tiled=True),
        (((1,), (1,)), ((), ())),
        preferred_element_type=jnp.float32,
    )
    grad_rows = lax.psum_scatter(partial_value, "pipe", scatter_dimension=0, tiled=True)
    count = grad_rows.shape[0]
    first = lax.axis_index("pipe") * count
    normed_rows = lax.dynamic_slice_in_dim(normed, first, count, 0)
    scale_rows = lax.dynamic_slice_in_dim(row_scale, first, count, 0)
    hidden_part, gain_part = norm_backward(grad_rows, normed_rows, scale_rows, gain)
    grad_hidden = lax.all_gather(hidden_part, "pipe", axis=0, tiled=True)
    gain_share = lax.psum_scatter(gain_part, "dp", scatter_dimension=0, tiled=True)
    gain_share = lax.psum(gain_share, "pipe")
    grad_gain = gain_share * average
    value_grad = (
        lax.psum_scatter(weight_term(encoded, cotangent), "dp", scatter_dimension=0, tiled=True)
        * average
    )
    return (grad_hidden, grad_gain, value_grad[None])


def solution(mesh):
    return jax.shard_map(
        local,
        mesh=mesh,
        in_specs=(P("dp", None), P(), P("pipe", "dp", None), P("pipe", "dp", None)),
        out_specs=(P("dp", None), P("dp"), P("pipe", "dp", None)),
        check_vma=False,
    )
```

profile of v0, /device:TPU:2, one launch (start us, length us, event | category | flops | bytes accessed | tf_op | source)
XLA Modules:
  0.0 277.6 jit_solution(11668662618033353739)
XLA Ops:
  7.2 0.0 copy-start
  7.2 0.0 all-gather.6.cloned.1.call-start
  7.2 0.7 all-gather.6.cloned.1.call-update
  7.9 0.0 reduce-scatter.3.cloned.1.call-start
  8.0 57.6 %all-gather.6.cloned.1.call-done = bf16[1,2048,2048]{2,1,0:T(8,128)(2,1)} async-done(((bf16[1,256,2048]{2,1,0:T(8,128)(2,1)}), bf16[1,2048,2048]{2,1,0:T(8,128)(2,1)}) %all-gather.6.cloned.1.call-update) | async-done | bytes 8388624 | tf_op jit(solution)/shard_map/all_gather | solution.py:33
  65.6 0.0 copy-done
  65.6 7.1 %fusion = f32[256,2048]{1,0:T(8,128)} fusion(bf16[1,2048,2048]{2,1,0:T(8,128)(2,1)} %all-gather.6.cloned.1.call-done, bf16[1,256,2048]{2,1,0:T(8,128)(2,1)S(1)} %copy-done), kind=kOutput, calls=%fused_computation | convolution fusion | flops 2147483648 | bytes 11534336 | tf_op jit(solution)/shard_map/dot_general | solution.py:31
  72.6 0.0 copy-start.1
  72.6 0.0 reduce-scatter.3.cloned.1.call-update
  72.6 0.0 all-gather.4.cloned.1.call-start
  72.7 1.1 copy-done.1
  73.8 0.0 copy-start.3
  73.8 0.3 fusion.2
  74.1 0.1 dynamic-slice.3
  74.2 1.6 convert_divide_fusion
  75.8 40.8 %reduce-scatter.3.cloned.1.call-done = f32[64,2048]{1,0:T(8,128)} async-done(((f32[256,2048]{1,0:T(8,128)}), f32[64,2048]{1,0:T(8,128)}) %reduce-scatter.3.cloned.1.call-update) | async-done | bytes 524304 | tf_op jit(solution)/shard_map/reduce_scatter | solution.py:37
  116.7 0.0 copy-done.3
  116.7 1.4 multiply_reduce_fusion
  118.1 2.0 divide_convert_fusion
  120.1 0.0 all-gather.4.cloned.1.call-update
  120.2 0.0 reduce-scatter.5.cloned.1.call-start
  120.2 8.3 %fusion.3 = f32[2048,2048]{1,0:T(8,128)} fusion(bf16[1,256,2048]{2,1,0:T(8,128)(2,1)S(1)} %copy-done, f32[2048]{0:T(1024)S(1)} %copy-done.3, bf16[256,2048]{1,0:T(8,128)(2,1)S(1)} %copy-done.1, f32[256]{0:T(256)S(1)} %add_sqrt_fusion), kind=kOutput, calls=%fused_computation.7 | convolution fusion | flops 2149580800 | bytes 18883584 | tf_op jit(solution)/shard_map/dot_general | solution.py:18
  128.5 0.0 copy-start.4
  128.5 0.0 reduce-scatter.5.cloned.1.call-update
  128.5 0.6 copy-done.4
  129.2 0.6 dynamic-slice.4
  130.4 11.5 %all-reduce = f32[2048]{0:T(1024)S(1)} all-reduce(f32[2048]{0:T(1024)S(1)} %get-tuple-element.3), channel_id=4, replica_groups=mesh['dp'=8,'pipe'=4] {'dp'}, use_global_device_ids=true, to_apply=%region_4.0.clone | all-reduce | flops 2048 | bytes 16384
  141.9 0.1 dynamic-slice.5
  142.0 10.1 %psum.7 = f32[256]{0:T(256)S(1)} all-reduce(f32[256]{0:T(256)S(1)} %dynamic-slice.5), channel_id=1, replica_groups=mesh['dp'=8,'pipe'=4] {'pipe'}, use_global_device_ids=true, to_apply=%region_5.0 | all-reduce | flops 256 | bytes 2048 | tf_op jit(solution)/shard_map/psum | solution.py:45
  152.1 0.6 broadcast_multiply_fusion
  152.7 0.0 all-gather.4.cloned.1.call-done
  152.7 0.0 copy-start.2
  152.7 114.3 %reduce-scatter.5.cloned.1.call-done = f32[256,2048]{1,0:T(8,128)} async-done(((f32[2048,2048]{1,0:T(8,128)}), f32[256,2048]{1,0:T(8,128)}) %reduce-scatter.5.cloned.1.call-update) | async-done | bytes 2097168 | tf_op jit(solution)/shard_map/reduce_scatter | solution.py:48
  267.0 3.1 %multiply_bitcast_fusion = f32[1,256,2048]{2,1,0:T(8,128)} fusion(f32[256,2048]{1,0:T(8,128)} %reduce-scatter.5.cloned.1.call-done), kind=kLoop, calls=%fused_computation.5 | loop fusion | flops 524288 | bytes 4194304 | tf_op jit(solution)/shard_map/broadcast_in_dim | solution.py:51
  270.1 0.0 copy-done.2
  270.1 1.0 copy.8
  (2 shorter events, 0.0 us)
Async XLA Ops:
  7.2 58.4 %copy-start = (bf16[1,256,2048]{2,1,0:T(8,128)(2,1)S(1)}, bf16[1,256,2048]{2,1,0:T(8,128)(2,1)}, u32[]{:S(2)}) copy-start(bf16[1,256,2048]{2,1,0:T(8,128)(2,1)} %param.7) | copy-start | bytes 3145732
  7.2 58.4 %all-gather.6.cloned.1.call-start = ((), (), s32[]{:S(2)}) async-start(), calls=%async_computation.5 | async-start | bytes 9437184 | tf_op jit(solution)/shard_map/all_gather | solution.py:33
  7.9 108.7 %reduce-scatter.3.cloned.1.call-start = ((), (), s32[]{:S(2)}) async-start(), calls=%async_computation.2 | async-start | bytes 2621440 | tf_op jit(solution)/shard_map/reduce_scatter | solution.py:37
  72.6 1.2 copy-start.1
  72.6 80.0 %all-gather.4.cloned.1.call-start = ((), (), s32[]{:S(2)}) async-start(), calls=%async_computation.3 | async-start | bytes 1310720 | tf_op jit(solution)/shard_map/all_gather | solution.py:43
  73.8 42.8 %copy-start.3 = (f32[2048]{0:T(1024)S(1)}, f32[2048]{0:T(1024)}, u32[]{:S(2)}) copy-start(f32[2048]{0:T(1024)} %param.5) | copy-start | bytes 24580
  120.2 146.8 %reduce-scatter.5.cloned.1.call-start = ((), (), s32[]{:S(2)}) async-start(), calls=%async_computation.4 | async-start | bytes 18874368 | tf_op jit(solution)/shard_map/reduce_scatter | solution.py:48
  128.5 0.7 copy-start.4
  152.7 117.5 %copy-start.2 = (bf16[256,2048]{1,0:T(8,128)(2,1)S(1)}, bf16[256,2048]{1,0:T(8,128)(2,1)}, u32[]{:S(2)}) copy-start(bf16[256,2048]{1,0:T(8,128)(2,1)} %all-gather.4.cloned.1.call-done) | copy-start | bytes 3145732
Sparse Core Ops, SparseCore 0:
  9.9 55.6 all-gather.5
  72.8 43.8 reduce-scatter.2
  120.3 27.6 all-gather.3
  151.9 115.0 reduce-scatter.4
where the time goes:
time: 280 us; the launch traced here: 278 us
  waiting for transfers between devices  213 us (76%)
  blocking collectives  21.6 us (8%)
  matrix products  15.4 us (6%)
  between operations  14.5 us (5%)
  other arithmetic  9.09 us (3%)
  local copies, waits for them, and re-layouts  3.5 us (1%)
    reduce_scatter x1, waiting for transfers between devices, local(): lax.psum_scatter(weight_term(encoded, cotangent), 'dp', scatter_dimension...  114 us
    all_gather x1, waiting for transfers between devices, local(): lax.all_gather(projection, 'dp', axis=0, tiled=True)  57.6 us
    reduce_scatter x1, waiting for transfers between devices, local(): lax.psum_scatter(partial_value, 'pipe', scatter_dimension=0, tiled=True)  40.8 us
    unnamed x1, blocking collectives  11.5 us
    psum x1, blocking collectives, local(): gain_share = lax.psum(gain_share, 'pipe')  10.1 us
    dot_general x1, matrix products, weight_term(): lax.dot_general(encoded, operand, (((0,), (0,)), ((), ())), preferred_ele...  8.32 us
    dot_general x1, matrix products, local(): lax.dot_general(cotangent, lax.all_gather(projection, 'dp', axis=0, tiled...  7.06 us
  transfers between devices with their start and end apart: 4, of which 3 were waited for; matrix products, arithmetic and copies ran while one was open for 4% of the time, Pallas kernels for 0%

commit v1 on v0

--- a/solution.py
+++ b/solution.py
@@ -1,9 +1,14 @@
+import functools
+
 import jax
 import jax.numpy as jnp
 from jax import lax
+from jax.experimental import pallas as pl
+from jax.experimental.pallas import tpu as pltpu
 from jax.sharding import PartitionSpec as P
 
 epsilon = 1e-06
+MESH = pl.DeviceIdType.MESH
 
 
 def norm_backward(grad_rows, normed_rows, scale_rows, gain):
@@ -20,7 +25,7 @@
     )
 
 
-def local(hidden, gain, w_value, d_value):
+def local_general(hidden, gain, w_value, d_value):
     hidden_f = hidden.astype(jnp.float32)
     row_scale = jnp.sqrt(jnp.mean(hidden_f * hidden_f, axis=-1, keepdims=True) + epsilon)
     normed = hidden_f / row_scale
@@ -51,7 +56,311 @@
     return (grad_hidden, grad_gain, value_grad[None])
 
 
+def kernel(
+    n_dp, n_pipe,
+    hidden_ref, gain_ref, w_ref, d_ref,
+    hidden_out, gain_out, value_out,
+    d_all, part, recv1, sum1, recv2, final, rows, enc, enc_cols, hid_all,
+    gain_part, gain_recv, gain_sum, gain_z,
+    own_sem, x_send, x_recv, y_send, y_recv, s_send, s_recv,
+    enc_send, enc_recv, one_send, one_recv, two_send, two_recv,
+    row_send, row_recv, hid_send, hid_recv, gp_send, gp_recv, gz_send, gz_recv,
+):
+    me = lax.axis_index("dp")
+    z = lax.axis_index("pipe")
+    core = me % 2
+    side_x = (me // 2) % 2
+    side_y = me // 4
+    step_s, step_x, step_y = 1 - 2 * core, 2 - 4 * side_x, 4 - 8 * side_y
+    at_s, at_x, at_y, at_d = me + step_s, me + step_x, me + step_y, me + step_x + step_y
+    parity, half_own = z % 2, z // 2
+    z_one = z + 1 - 2 * parity
+    z_two = z + 2 - 4 * half_own
+    chunk, width = rows.shape[1], rows.shape[2]
+    model = gain_ref.shape[-1]
+
+    barrier = pltpu.get_barrier_semaphore()
+    for k in range(1, n_dp):
+        pl.semaphore_signal(barrier, inc=1, device_id=((me + k) % n_dp, z), device_id_type=MESH)
+    for other in (z_one, z_two):
+        pl.semaphore_signal(barrier, inc=1, device_id=(me, other), device_id_type=MESH)
+    pl.semaphore_wait(barrier, n_dp - 1 + 2)
+
+    sent = []
+
+    def send(src, dst, send_sem, recv_sem, target):
+        copy = pltpu.make_async_remote_copy(
+            src_ref=src, dst_ref=dst, send_sem=send_sem, recv_sem=recv_sem,
+            device_id=target, device_id_type=MESH,
+        )
+        copy.start()
+        sent.append(copy)
+
+    def arrived(dst, recv_sem):
+        pltpu.make_async_remote_copy(
+            src_ref=dst, dst_ref=dst, send_sem=recv_sem, recv_sem=recv_sem,
+            device_id=(me, z_one), device_id_type=MESH,
+        ).wait_recv()
+
+    send(d_ref.at[0], d_all.at[me, 0], x_send.at[0], x_recv.at[0], (at_x, z))
+    send(d_ref.at[1], d_all.at[me, 1], y_send.at[1], y_recv.at[1], (at_y, z))
+    send(d_ref.at[0], d_all.at[me, 0], s_send.at[0, 0], s_recv.at[0, 0], (at_s, z))
+    send(d_ref.at[1], d_all.at[me, 1], s_send.at[0, 1], s_recv.at[0, 1], (at_s, z))
+    send(d_ref.at[1], d_all.at[me, 1], x_send.at[1], x_recv.at[1], (at_x, z))
+    send(d_ref.at[0], d_all.at[me, 0], y_send.at[0], y_recv.at[0], (at_y, z))
+    own = pltpu.make_async_copy(d_ref, d_all.at[me], own_sem)
+    own.start()
+
+    def process(block, origin, half):
+        product = lax.dot_general(
+            block, w_ref[...], (((1,), (1,)), ((), ())), preferred_element_type=jnp.float32
+        )
+        part[origin, half] = product.reshape(2, chunk, width)
+        send(
+            part.at[origin, half, 1 - parity], recv1.at[origin, half],
+            one_send.at[origin, half], one_recv.at[origin, half], (me, z_one),
+        )
+
+    def arrive_process(origin, half):
+        process(d_all[origin, half], origin, half)
+
+    def share(kind, origin, half):
+        send(
+            d_all.at[origin, half], d_all.at[origin, half],
+            s_send.at[kind, half], s_recv.at[kind, half], (at_s, z),
+        )
+
+    def first_sum(origin):
+        for half, goes in ((1 - half_own, True), (half_own, False)):
+            arrived(recv1.at[origin, half], one_recv.at[origin, half])
+            total = part[origin, half, parity] + recv1[origin, half]
+            if goes:
+                sum1[origin] = total
+                send(
+                    sum1.at[origin], recv2.at[origin],
+                    two_send.at[origin], two_recv.at[origin], (me, z_two),
+                )
+            else:
+                part[origin, half, parity] = total
+
+    def second_sum(origin, mine):
+        arrived(recv2.at[origin], two_recv.at[origin])
+        total = part[origin, half_own, parity] + recv2[origin]
+        if mine:
+            rows[me] = total
+        else:
+            final[origin] = total
+            send(
+                final.at[origin], rows.at[me],
+                row_send.at[origin], row_recv.at[me], (origin, z),
+            )
+
+    process(d_ref[0], me, 0)
+    process(d_ref[1], me, 1)
+    for half in range(2):
+        arrived(d_all.at[at_s, half], s_recv.at[0, half])
+        arrive_process(at_s, half)
+
+    def scale_of(block):
+        return jnp.sqrt(jnp.mean(block * block, axis=-1, keepdims=True) + epsilon)
+
+    for q in range(n_pipe):
+        block = hidden_ref[q].astype(jnp.float32)
+        value = (block * (1.0 / scale_of(block)) * gain_ref[...]).astype(jnp.bfloat16)
+        for j in range(n_dp):
+            enc[j, q] = value[:, j * width:(j + 1) * width]
+    enc_cols[me] = enc[me]
+
+    arrived(d_all.at[at_x, 0], x_recv.at[0])
+    send(d_all.at[at_x, 0], d_all.at[at_x, 0], y_send.at[2], y_recv.at[2], (at_y, z))
+    share(1, at_x, 0)
+    arrived(d_all.at[at_y, 1], y_recv.at[1])
+    send(d_all.at[at_y, 1], d_all.at[at_y, 1], x_send.at[2], x_recv.at[2], (at_x, z))
+    share(2, at_y, 1)
+    arrive_process(at_x, 0)
+    arrive_process(at_y, 1)
+    arrived(d_all.at[at_x + step_s, 0], s_recv.at[1, 0])
+    arrive_process(at_x + step_s, 0)
+    arrived(d_all.at[at_y + step_s, 1], s_recv.at[2, 1])
+    arrive_process(at_y + step_s, 1)
+    first_sum(me)
+    first_sum(at_s)
+
+    arrived(d_all.at[at_x, 1], x_recv.at[1])
+    share(1, at_x, 1)
+    arrived(d_all.at[at_y, 0], y_recv.at[0])
+    share(2, at_y, 0)
+    for k in range(1, n_dp):
+        to = (me + k) % n_dp
+        send(enc.at[to], enc_cols.at[me], enc_send.at[to], enc_recv.at[me], (to, z))
+    arrive_process(at_x, 1)
+    arrive_process(at_y, 0)
+    arrived(d_all.at[at_x + step_s, 1], s_recv.at[1, 1])
+    arrive_process(at_x + step_s, 1)
+    arrived(d_all.at[at_y + step_s, 0], s_recv.at[2, 0])
+    arrive_process(at_y + step_s, 0)
+    second_sum(me, True)
+    second_sum(at_s, False)
+    for origin in (at_x, at_y, at_x + step_s, at_y + step_s):
+        first_sum(origin)
+
+    arrived(d_all.at[at_d, 0], y_recv.at[2])
+    share(3, at_d, 0)
+    arrived(d_all.at[at_d, 1], x_recv.at[2])
+    share(3, at_d, 1)
+    arrive_process(at_d, 0)
+    arrive_process(at_d, 1)
+    for half in range(2):
+        arrived(d_all.at[at_d + step_s, half], s_recv.at[3, half])
+        arrive_process(at_d + step_s, half)
+    for origin in (at_x, at_y, at_x + step_s, at_y + step_s):
+        second_sum(origin, False)
+    first_sum(at_d)
+    first_sum(at_d + step_s)
+    second_sum(at_d, False)
+    second_sum(at_d + step_s, False)
+
+    block = hidden_ref[z].astype(jnp.float32)
+    inverse = 1.0 / scale_of(block)
+    for k in range(1, n_dp):
+        source = (me + k) % n_dp
+        arrived(rows.at[source], row_recv.at[source])
+    dots = jnp.zeros((chunk, 1), jnp.float32)
+    for j in range(n_dp):
+        columns = slice(j * width, (j + 1) * width)
+        normed = hidden_ref[z, :, columns].astype(jnp.float32) * inverse
+        product = rows[j] * normed
+        dots += jnp.sum(product * gain_ref[:, columns], axis=-1, keepdims=True)
+        gain_part[j] = jnp.sum(product.reshape(chunk // 8, 8, width), axis=0)
+    dots = dots * (1.0 / model)
+    for j in range(n_dp):
+        columns = slice(j * width, (j + 1) * width)
+        normed = hidden_ref[z, :, columns].astype(jnp.float32) * inverse
+        scaled = rows[j] * gain_ref[:, columns]
+        hid_all[z, :, columns] = ((scaled - normed * dots) * inverse).astype(jnp.bfloat16)
+    send(hid_all.at[z], hid_all.at[z], hid_send.at[0], hid_recv.at[0], (me, z_two))
+    send(hid_all.at[z], hid_all.at[z], hid_send.at[1], hid_recv.at[1], (me, z_one))
+    gain_recv[me] = gain_part[me]
+    for k in range(1, n_dp):
+        to = (me + k) % n_dp
+        send(gain_part.at[to], gain_recv.at[me], gp_send.at[to], gp_recv.at[me], (to, z))
+
+    for k in range(1, n_dp):
+        source = (me + k) % n_dp
+        arrived(enc_cols.at[source], enc_recv.at[source])
+    own.wait()
+    count = n_dp * 2 * d_all.shape[2]
+    tile = 2 * width
+
+    def value_tiles(first, last):
+        def body(t, carry):
+            columns = pl.ds(pl.multiple_of(t * tile, tile), tile)
+            value_out[:, columns] = lax.dot_general(
+                enc_cols[...].reshape(count, width),
+                d_all[:, :, :, columns].reshape(count, tile),
+                (((0,), (0,)), ((), ())),
+                preferred_element_type=jnp.float32,
+            )
+            return carry
+
+        lax.fori_loop(first, last, body, 0)
+
+    tiles = d_all.shape[-1] // tile
+    for k in range(1, n_dp):
+        source = (me + k) % n_dp
+        arrived(gain_recv.at[source], gp_recv.at[source])
+    gain_sum[0] = jnp.sum(gain_recv[...], axis=0)
+    send(gain_sum.at[0], gain_z.at[0], gz_send.at[0], gz_recv.at[0], (me, z_one))
+    value_tiles(0, tiles // 2)
+    arrived(gain_z.at[0], gz_recv.at[0])
+    gain_sum[1] = gain_sum[0] + gain_z[0]
+    send(gain_sum.at[1], gain_z.at[1], gz_send.at[1], gz_recv.at[1], (me, z_two))
+    arrived(hid_all.at[z_two], hid_recv.at[0])
+    send(hid_all.at[z_two], hid_all.at[z_two], hid_send.at[2], hid_recv.at[2], (me, z_one))
+    value_tiles(tiles // 2, tiles)
+    arrived(gain_z.at[1], gz_recv.at[1])
+    gain_out[...] = jnp.sum(gain_sum[1] + gain_z[1], axis=0, keepdims=True) * (1.0 / n_dp)
+    arrived(hid_all.at[z_one], hid_recv.at[1])
+    arrived(hid_all.at[z_one + z_two - z], hid_recv.at[2])
+    hidden_out[...] = hid_all[...]
+    for copy in sent:
+        copy.wait_send()
+
+
+def local_cube(n_dp, n_pipe, hidden, gain, w_value, d_value):
+    tokens, model = hidden.shape
+    kv = d_value.shape[-1]
+    width = w_value.shape[1]
+    chunk = tokens // n_pipe
+    f32, bf16 = jnp.float32, jnp.bfloat16
+    dma = pltpu.SemaphoreType.DMA
+    vmem = pl.BlockSpec(memory_space=pltpu.VMEM)
+    flops = 4 * n_dp * tokens * width * kv
+    hidden_grad, gain_grad, value_grad = pl.pallas_call(
+        functools.partial(kernel, n_dp, n_pipe),
+        out_shape=(
+            jax.ShapeDtypeStruct((n_pipe, chunk, model), bf16),
+            jax.ShapeDtypeStruct((1, width), f32),
+            jax.ShapeDtypeStruct((width, kv), f32),
+        ),
+        in_specs=[vmem] * 4,
+        out_specs=(vmem, vmem, vmem),
+        scratch_shapes=[
+            pltpu.VMEM((n_dp, 2, 2 * chunk, kv), bf16),
+            pltpu.VMEM((n_dp, 2, 2, chunk, width), f32),
+            pltpu.VMEM((n_dp, 2, chunk, width), f32),
+            pltpu.VMEM((n_dp, chunk, width), f32),
+            pltpu.VMEM((n_dp, chunk, width), f32),
+            pltpu.VMEM((n_dp, chunk, width), f32),
+            pltpu.VMEM((n_dp, chunk, width), f32),
+            pltpu.VMEM((n_dp, n_pipe, chunk, width), bf16),
+            pltpu.VMEM((n_dp, n_pipe, chunk, width), bf16),
+            pltpu.VMEM((n_pipe, chunk, model), bf16),
+            pltpu.VMEM((n_dp, 8, width), f32),
+            pltpu.VMEM((n_dp, 8, width), f32),
+            pltpu.VMEM((2, 8, width), f32),
+            pltpu.VMEM((2, 8, width), f32),
+            dma(()),
+            dma((3,)), dma((3,)), dma((3,)), dma((3,)),
+            dma((4, 2)), dma((4, 2)),
+            dma((n_dp,)), dma((n_dp,)),
+            dma((n_dp, 2)), dma((n_dp, 2)),
+            dma((n_dp,)), dma((n_dp,)),
+            dma((n_dp,)), dma((n_dp,)),
+            dma((3,)), dma((3,)),
+            dma((n_dp,)), dma((n_dp,)),
+            dma((2,)), dma((2,)),
+        ],
+        compiler_params=pltpu.CompilerParams(
+            collective_id=0, has_side_effects=True, vmem_limit_bytes=50 * 2**20
+        ),
+        cost_estimate=pl.CostEstimate(flops=flops, bytes_accessed=8 * 2**20, transcendentals=0),
+    )(
+        hidden.reshape(n_pipe, chunk, model),
+        gain.reshape(1, model),
+        w_value[0],
+        d_value[0].reshape(2, 2 * chunk, kv),
+    )
+    return (
+        hidden_grad.reshape(tokens, model),
+        gain_grad.reshape(width),
+        (value_grad * (1.0 / n_dp))[None],
+    )
+
+
 def solution(mesh):
+    n_dp, n_pipe = mesh.shape["dp"], mesh.shape["pipe"]
+
+    def local(hidden, gain, w_value, d_value):
+        tokens, model = hidden.shape
+        width = w_value.shape[1]
+        cube = n_dp == 2 * 2 * 2 and n_pipe == 2 * 2
+        fits = tokens % (16 * n_pipe) == 0 and width % 128 == 0 and model == n_dp * width
+        fits = fits and d_value.shape[-1] % (4 * width) == 0 and n_dp * tokens <= model
+        if cube and fits:
+            return local_cube(n_dp, n_pipe, hidden, gain, w_value, d_value)
+        return local_general(hidden, gain, w_value, d_value)
+
     return jax.shard_map(
         local,
         mesh=mesh,

time: 280 us -> 95 us (0.34)
  waiting for transfers between devices: 213 us -> 0 us
  Pallas kernels: 0 us -> 86.2 us
  blocking collectives: 21.6 us -> 0 us
  matrix products: 15.4 us -> 0 us
  between operations: 14.5 us -> 0.65 us
  other arithmetic: 9.09 us -> 3.14 us
    reduce_scatter x2 -> x0, waiting for transfers between devices: 155 us -> none  [the longest x1 114 us: local(): lax.psum_scatter(weight_term(encoded, cotangent), 'dp', scatter_dimension...]
    pallas_call x0 -> x1, Pallas kernels: none -> 86.2 us  [local_cube(): pl.pallas_call(functools.partial(kernel, n_dp, n_pipe), out_shape=(jax.Sh...]
    all_gather x2 -> x0, waiting for transfers between devices: 57.6 us -> none  [the longest x1 57.6 us: local(): lax.all_gather(projection, 'dp', axis=0, tiled=True)]
    dot_general x2 -> x0, matrix products: 15.4 us -> none  [the longest x1 8.32 us: weight_term(): lax.dot_general(encoded, operand, (((0,), (0,)), ((), ())), preferred_ele...]
    unnamed x1 -> x0, blocking collectives: 11.5 us -> none
    psum x1 -> x0, blocking collectives: 10.1 us -> none  [local(): gain_share = lax.psum(gain_share, 'pipe')]
  transfers between devices with their start and end apart: 4 -> 0, of which waited for: 3 -> 0; matrix products, arithmetic and copies ran while one was open for 4% -> 0% of each run, Pallas kernels for 0% -> 0%
where the time goes in v1:
time: 95 us; the launch traced here: 94.7 us
  Pallas kernels  86.2 us (91%)
  local copies, waits for them, and re-layouts  4.67 us (5%)
  other arithmetic  3.14 us (3%)
    pallas_call x1, Pallas kernels, local_cube(): pl.pallas_call(functools.partial(kernel, n_dp, n_pipe), out_shape=(jax.Sh...  86.2 us
    unnamed x8, local copies, waits for them, and re-layouts  4.67 us
    broadcast_in_dim x1, other arithmetic, local_cube(): (value_grad * (1.0 / n_dp))[None]  3.14 us

profile of v1, /device:TPU:2, one launch (start us, length us, event | category | flops | bytes accessed | tf_op | source)
XLA Modules:
  0.0 94.7 jit_solution(7908344779133053154)
XLA Ops:
  0.6 0.0 copy-start
  0.6 1.2 %copy-done = bf16[256,2048]{1,0:T(8,128)(2,1)S(1)} copy-done((bf16[256,2048]{1,0:T(8,128)(2,1)S(1)}, bf16[256,2048]{1,0:T(8,128)(2,1)}, u32[]{:S(2)}) %copy-start) | copy-done | bytes 1048600
  1.9 0.0 copy-start.1
  1.9 1.2 %copy-done.1 = bf16[1,256,2048]{2,1,0:T(8,128)(2,1)S(1)} copy-done((bf16[1,256,2048]{2,1,0:T(8,128)(2,1)S(1)}, bf16[1,256,2048]{2,1,0:T(8,128)(2,1)}, u32[]{:S(2)}) %copy-start.1) | copy-done | bytes 1048600
  3.1 0.0 copy-start.2
  3.1 0.7 copy-done.2
  3.8 86.2 %shard_map.67 = (bf16[4,64,2048]{2,1,0:T(8,128)(2,1)S(1)}, f32[1,256]{1,0:T(1,128)S(1)}, f32[256,2048]{1,0:T(8,128)}) custom-call(bf16[4,64,2048]{2,1,0:T(8,128)(2,1)S(1)} %bitcast.10, f32[1,2048]{1,0:T(1,128)S(1)} %bitcast.12, bf16[256,2048]{1,0:T(8,128)(2,1)S(1)} %bitcast.11, bf16[2,128,2048]{2,1,0:T(8,128)(2,1)} %bitcast.13), custom_call_target="tpu_custom_call" | custom-call | flops 4294967296 | bytes 8388608 | tf_op jit(solution)/shard_map/pallas_call | solution.py:299
  90.0 3.1 %multiply_bitcast_fusion = f32[1,256,2048]{2,1,0:T(8,128)} fusion(f32[256,2048]{1,0:T(8,128)} %get-tuple-element.8), kind=kLoop, calls=%fused_computation | loop fusion | flops 524288 | bytes 4194304 | tf_op jit(solution)/shard_map/broadcast_in_dim | solution.py:347
  93.2 1.0 %copy.9 = bf16[256,2048]{1,0:T(8,128)(2,1)} copy(bf16[256,2048]{1,0:T(8,128)(2,1)S(1)} %bitcast.8) | data formatting | bytes 2097152
  94.2 0.6 copy.10
Async XLA Ops:
  0.6 1.2 %copy-start = (bf16[256,2048]{1,0:T(8,128)(2,1)S(1)}, bf16[256,2048]{1,0:T(8,128)(2,1)}, u32[]{:S(2)}) copy-start(bf16[256,2048]{1,0:T(8,128)(2,1)} %param.4) | copy-start | bytes 3145732
  1.9 1.2 %copy-start.1 = (bf16[1,256,2048]{2,1,0:T(8,128)(2,1)S(1)}, bf16[1,256,2048]{2,1,0:T(8,128)(2,1)}, u32[]{:S(2)}) copy-start(bf16[1,256,2048]{2,1,0:T(8,128)(2,1)} %param.6) | copy-start | bytes 3145732
  3.1 0.7 copy-start.2

commit v2 on v0

--- a/solution.py
+++ b/solution.py
@@ -1,9 +1,14 @@
+import functools
+
 import jax
 import jax.numpy as jnp
 from jax import lax
+from jax.experimental import pallas as pl
+from jax.experimental.pallas import tpu as pltpu
 from jax.sharding import PartitionSpec as P
 
 epsilon = 1e-06
+MESH = pl.DeviceIdType.MESH
 
 
 def norm_backward(grad_rows, normed_rows, scale_rows, gain):
@@ -20,7 +25,7 @@
     )
 
 
-def local(hidden, gain, w_value, d_value):
+def local_general(hidden, gain, w_value, d_value):
     hidden_f = hidden.astype(jnp.float32)
     row_scale = jnp.sqrt(jnp.mean(hidden_f * hidden_f, axis=-1, keepdims=True) + epsilon)
     normed = hidden_f / row_scale
@@ -51,7 +56,388 @@
     return (grad_hidden, grad_gain, value_grad[None])
 
 
+def kernel(
+    n_dp, n_pipe,
+    hidden_hbm, gain_hbm, w_hbm, d_hbm,
+    hidden_out, gain_out, value_out,
+    hidden_ref, gain_ref, w_ref, value_ref,
+    d_all, part, out1, recv1, sum1, recv2, final, rows, enc, enc_cols,
+    gain_part, gain_recv, gain_sum, gain_z,
+    own_sem, x_send, x_recv, y_send, y_recv, s_send, s_recv,
+    enc_send, enc_recv, one_send, one_recv, two_send, two_recv,
+    row_send, row_recv, hid_send, hid_recv, gp_send, gp_recv, gz_send, gz_recv,
+):
+    me = lax.axis_index("dp")
+    z = lax.axis_index("pipe")
+    core = me % 2
+    side_x = (me // 2) % 2
+    side_y = me // 4
+    step_s, step_x, step_y = 1 - 2 * core, 2 - 4 * side_x, 4 - 8 * side_y
+    at_s, at_x, at_y, at_d = me + step_s, me + step_x, me + step_y, me + step_x + step_y
+    parity, half_own = z % 2, z // 2
+    z_one = z + 1 - 2 * parity
+    z_two = z + 2 - 4 * half_own
+    chunk, width = rows.shape[2], rows.shape[3]
+    model = gain_ref.shape[-1]
+
+    own = pltpu.make_async_copy(d_hbm, d_all.at[me], own_sem.at[0])
+    load_w = pltpu.make_async_copy(w_hbm, w_ref, own_sem.at[1])
+    load_h = pltpu.make_async_copy(hidden_hbm, hidden_ref, own_sem.at[2])
+    load_g = pltpu.make_async_copy(gain_hbm, gain_ref, own_sem.at[3])
+    for copy in (own, load_w, load_h, load_g):
+        copy.start()
+
+    barrier = pltpu.get_barrier_semaphore()
+    for k in range(1, n_dp):
+        pl.semaphore_signal(barrier, inc=1, device_id=((me + k) % n_dp, z), device_id_type=MESH)
+    for other in (z_one, z_two):
+        pl.semaphore_signal(barrier, inc=1, device_id=(me, other), device_id_type=MESH)
+    pl.semaphore_wait(barrier, n_dp - 1 + 2)
+
+    sent = []
+
+    def send(src, dst, send_sem, recv_sem, target):
+        copy = pltpu.make_async_remote_copy(
+            src_ref=src, dst_ref=dst, send_sem=send_sem, recv_sem=recv_sem,
+            device_id=target, device_id_type=MESH,
+        )
+        copy.start()
+        sent.append(copy)
+
+    def arrived(dst, recv_sem):
+        pltpu.make_async_remote_copy(
+            src_ref=dst, dst_ref=dst, send_sem=recv_sem, recv_sem=recv_sem,
+            device_id=(me, z_one), device_id_type=MESH,
+        ).wait_recv()
+
+    def own_x(sub, half):
+        send(d_hbm.at[sub, half], d_all.at[me, sub, half],
+             x_send.at[sub, half], x_recv.at[sub, half], (at_x, z))
+
+    def own_y(sub, half):
+        send(d_hbm.at[sub, half], d_all.at[me, sub, half],
+             y_send.at[sub, half], y_recv.at[sub, half], (at_y, z))
+
+    def own_s(sub, half):
+        send(d_hbm.at[sub, half], d_all.at[me, sub, half],
+             s_send.at[sub, 0, half], s_recv.at[sub, 0, half], (at_s, z))
+
+    def share(sub, kind, origin, half):
+        send(d_all.at[origin, sub, half], d_all.at[origin, sub, half],
+             s_send.at[sub, kind, half], s_recv.at[sub, kind, half], (at_s, z))
+
+    def product(sub, *blocks):
+        joined = jnp.concatenate([d_all[origin, sub, half] for origin, half in blocks], axis=0)
+        result = lax.dot_general(
+            joined, w_ref[...], (((1,), (1,)), ((), ())), preferred_element_type=jnp.float32
+        )
+        count = 2 * chunk
+        for k, (origin, half) in enumerate(blocks):
+            part[origin, sub, half] = result[k * count:(k + 1) * count].reshape(2, chunk, width)
+            out1[origin, sub, half] = part[origin, sub, half, 1 - parity].astype(jnp.bfloat16)
+            send(
+                out1.at[origin, sub, half], recv1.at[origin, sub, half],
+                one_send.at[origin, sub, half], one_recv.at[origin, sub, half], (me, z_one),
+            )
+
+    def first_sum(sub, *origins):
+        for origin in origins:
+            goes, stays = 1 - half_own, half_own
+            arrived(recv1.at[origin, sub, goes], one_recv.at[origin, sub, goes])
+            sum1[origin, sub] = (
+                part[origin, sub, goes, parity] + recv1[origin, sub, goes].astype(jnp.float32)
+            )
+            send(
+                sum1.at[origin, sub], recv2.at[origin, sub],
+                two_send.at[origin, sub], two_recv.at[origin, sub], (me, z_two),
+            )
+            arrived(recv1.at[origin, sub, stays], one_recv.at[origin, sub, stays])
+
+    def second_sum(sub, *origins):
+        for origin in origins:
+            arrived(recv2.at[origin, sub], two_recv.at[origin, sub])
+            kept = recv1[origin, sub, half_own].astype(jnp.float32)
+            total = part[origin, sub, half_own, parity] + kept + recv2[origin, sub]
+            if origin is me:
+                rows[me, sub] = total
+            else:
+                final[origin, sub] = total
+                send(
+                    final.at[origin, sub], rows.at[me, sub],
+                    row_send.at[origin, sub], row_recv.at[me, sub], (origin, z),
+                )
+
+    def scale_of(block):
+        return jnp.sqrt(jnp.mean(block * block, axis=-1, keepdims=True) + epsilon)
+
+    def gather_first(sub):
+        arrived(d_all.at[at_x, sub, 0], x_recv.at[sub, 0])
+        send(d_all.at[at_x, sub, 0], d_all.at[at_x, sub, 0],
+             y_send.at[sub, 2], y_recv.at[sub, 2], (at_y, z))
+        share(sub, 1, at_x, 0)
+        arrived(d_all.at[at_y, sub, 1], y_recv.at[sub, 1])
+        send(d_all.at[at_y, sub, 1], d_all.at[at_y, sub, 1],
+             x_send.at[sub, 2], x_recv.at[sub, 2], (at_x, z))
+        share(sub, 2, at_y, 1)
+
+    def gather_second(sub):
+        arrived(d_all.at[at_x, sub, 1], x_recv.at[sub, 1])
+        share(sub, 1, at_x, 1)
+        arrived(d_all.at[at_y, sub, 0], y_recv.at[sub, 0])
+        share(sub, 2, at_y, 0)
+
+    def gather_third(sub):
+        arrived(d_all.at[at_d, sub, 0], y_recv.at[sub, 2])
+        share(sub, 3, at_d, 0)
+        arrived(d_all.at[at_d, sub, 1], x_recv.at[sub, 2])
+        share(sub, 3, at_d, 1)
+
+    def products(sub, *kinds):
+        product(sub, *[((at_x, at_y, at_d)[kind - 1], half) for kind, half in kinds])
+        siblings = [((at_x, at_y, at_d)[kind - 1] + step_s, half) for kind, half in kinds]
+        for (kind, half), (origin, _) in zip(kinds, siblings):
+            arrived(d_all.at[origin, sub, half], s_recv.at[sub, kind, half])
+        product(sub, *siblings)
+
+    sides = (at_x, at_y, at_x + step_s, at_y + step_s)
+    corners = (at_d, at_d + step_s)
+    pair = (me, at_s)
+
+    def send_encoded(*targets):
+        for to in targets:
+            send(enc.at[to], enc_cols.at[me], enc_send.at[to], enc_recv.at[me], (to, z))
+
+    def norm_part(sub):
+        block = hidden_ref[sub, z].astype(jnp.float32)
+        inverse = 1.0 / scale_of(block)
+        for k in range(1, n_dp):
+            source = (me + k) % n_dp
+            arrived(rows.at[source, sub], row_recv.at[source, sub])
+        dots = jnp.zeros((chunk, 1), jnp.float32)
+        for j in range(n_dp):
+            columns = slice(j * width, (j + 1) * width)
+            normed = hidden_ref[sub, z, :, columns].astype(jnp.float32) * inverse
+            term = rows[j, sub] * normed
+            dots += jnp.sum(term * gain_ref[:, columns], axis=-1, keepdims=True)
+            folded = jnp.sum(term.reshape(chunk // 8, 8, width), axis=0)
+            gain_part[j] = folded if sub == 0 else gain_part[j] + folded
+        dots = dots * (1.0 / model)
+        for j in range(n_dp):
+            columns = slice(j * width, (j + 1) * width)
+            normed = hidden_ref[sub, z, :, columns].astype(jnp.float32) * inverse
+            scaled = rows[j, sub] * gain_ref[:, columns]
+            hidden_out[sub, z, :, columns] = ((scaled - normed * dots) * inverse).astype(
+                jnp.bfloat16
+            )
+        mine = hidden_out.at[sub, z]
+        send(mine, mine, hid_send.at[sub, 0], hid_recv.at[sub, 0], (me, z_two))
+        send(mine, mine, hid_send.at[sub, 1], hid_recv.at[sub, 1], (me, z_one))
+
+    def norm_pass_on(sub):
+        theirs = hidden_out.at[sub, z_two]
+        arrived(theirs, hid_recv.at[sub, 0])
+        send(theirs, theirs, hid_send.at[sub, 2], hid_recv.at[sub, 2], (me, z_one))
+
+    def norm_end(sub):
+        arrived(hidden_out.at[sub, z_one], hid_recv.at[sub, 1])
+        arrived(hidden_out.at[sub, z_one + z_two - z], hid_recv.at[sub, 2])
+
+    own_x(0, 0)
+    own_y(0, 1)
+    own_s(0, 0)
+    own_s(0, 1)
+    own_x(0, 1)
+    own_y(0, 0)
+    own_s(1, 0)
+    own_s(1, 1)
+    load_w.wait()
+    own.wait()
+    for sub in range(2):
+        product(sub, (me, 0), (me, 1))
+        for half in range(2):
+            arrived(d_all.at[at_s, sub, half], s_recv.at[sub, 0, half])
+        product(sub, (at_s, 0), (at_s, 1))
+
+    load_h.wait()
+    load_g.wait()
+    for sub in range(2):
+        for q in range(n_pipe):
+            block = hidden_ref[sub, q].astype(jnp.float32)
+            value = (block * (1.0 / scale_of(block)) * gain_ref[...]).astype(jnp.bfloat16)
+            for j in range(n_dp):
+                enc[j, sub, q] = value[:, j * width:(j + 1) * width]
+    enc_cols[me] = enc[me]
+    send_encoded(at_s)
+
+    gather_first(0)
+    own_x(1, 0)
+    own_y(1, 1)
+    products(0, (1, 0), (2, 1))
+    gather_second(0)
+    own_x(1, 1)
+    own_y(1, 0)
+    products(0, (1, 1), (2, 0))
+    first_sum(0, *pair)
+    gather_third(0)
+    products(0, (3, 0), (3, 1))
+    gather_first(1)
+    products(1, (1, 0), (2, 1))
+    first_sum(0, *sides)
+    second_sum(0, *pair)
+    gather_second(1)
+    products(1, (1, 1), (2, 0))
+    first_sum(0, *corners)
+    first_sum(1, *pair)
+    second_sum(0, *sides)
+    second_sum(0, *corners)
+    first_sum(1, *sides)
+    second_sum(1, *pair)
+    gather_third(1)
+    products(1, (3, 0), (3, 1))
+    send_encoded(*sides)
+    norm_part(0)
+    first_sum(1, *corners)
+    second_sum(1, *sides)
+    norm_pass_on(0)
+    second_sum(1, *corners)
+    send_encoded(*corners)
+    norm_part(1)
+    gain_recv[me] = gain_part[me]
+    for k in range(1, n_dp):
+        to = (me + k) % n_dp
+        send(gain_part.at[to], gain_recv.at[me], gp_send.at[to], gp_recv.at[me], (to, z))
+
+    count = 2 * enc_cols.shape[1] * enc_cols.shape[2] * enc_cols.shape[3]
+    tile = 2 * width
+    tiles = d_all.shape[-1] // tile
+    stores = []
+
+    def value_term(step, near, far):
+        for source in (near, far):
+            if source is not me:
+                arrived(enc_cols.at[source], enc_recv.at[source])
+        encoded = jnp.concatenate(
+            [enc_cols[source].reshape(count // 2, width) for source in (near, far)], axis=0
+        )
+        for t in range(tiles):
+            columns = slice(t * tile, (t + 1) * tile)
+            operand = jnp.concatenate(
+                [d_all[source, :, :, :, columns].reshape(count // 2, tile) for source in (near, far)],
+                axis=0,
+            )
+            term = lax.dot_general(
+                encoded, operand, (((0,), (0,)), ((), ())), preferred_element_type=jnp.float32
+            )
+            if step > 0:
+                term = value_ref[:, columns] + term
+            if step < 3:
+                value_ref[:, columns] = term
+            else:
+                value_ref[:, columns] = term * (1.0 / n_dp)
+                store = pltpu.make_async_copy(
+                    value_ref.at[:, columns], value_out.at[:, columns], own_sem.at[4 + t]
+                )
+                store.start()
+                stores.append(store)
+
+    value_term(0, me, at_s)
+    for k in range(1, n_dp):
+        source = (me + k) % n_dp
+        arrived(gain_recv.at[source], gp_recv.at[source])
+    gain_sum[0] = jnp.sum(gain_recv[...], axis=0)
+    send(gain_sum.at[0], gain_z.at[0], gz_send.at[0], gz_recv.at[0], (me, z_one))
+    value_term(1, at_x, at_x + step_s)
+    arrived(gain_z.at[0], gz_recv.at[0])
+    gain_sum[1] = gain_sum[0] + gain_z[0]
+    send(gain_sum.at[1], gain_z.at[1], gz_send.at[1], gz_recv.at[1], (me, z_two))
+    value_term(2, at_y, at_y + step_s)
+    norm_pass_on(1)
+    value_term(3, at_d, at_d + step_s)
+    arrived(gain_z.at[1], gz_recv.at[1])
+    gain_out[...] = jnp.sum(gain_sum[1] + gain_z[1], axis=0, keepdims=True) * (1.0 / n_dp)
+    norm_end(0)
+    norm_end(1)
+    for copy in sent:
+        copy.wait_send()
+    for store in stores:
+        store.wait()
+
+
+def local_cube(n_dp, n_pipe, hidden, gain, w_value, d_value):
+    tokens, model = hidden.shape
+    kv = d_value.shape[-1]
+    width = w_value.shape[1]
+    chunk = tokens // (2 * n_pipe)
+    f32, bf16 = jnp.float32, jnp.bfloat16
+    dma = pltpu.SemaphoreType.DMA
+    vmem = pl.BlockSpec(memory_space=pltpu.VMEM)
+    hbm = pl.BlockSpec(memory_space=pltpu.HBM)
+    flops = 4 * n_dp * tokens * width * kv
+    hidden_grad, gain_grad, value_grad = pl.pallas_call(
+        functools.partial(kernel, n_dp, n_pipe),
+        out_shape=(
+            jax.ShapeDtypeStruct((2, n_pipe, chunk, model), bf16),
+            jax.ShapeDtypeStruct((1, width), f32),
+            jax.ShapeDtypeStruct((width, kv), f32),
+        ),
+        in_specs=[hbm] * 4,
+        out_specs=(vmem, vmem, hbm),
+        scratch_shapes=[
+            pltpu.VMEM((2, n_pipe, chunk, model), bf16),
+            pltpu.VMEM((1, model), f32),
+            pltpu.VMEM((width, kv), bf16),
+            pltpu.VMEM((width, kv), f32),
+            pltpu.VMEM((n_dp, 2, 2, 2 * chunk, kv), bf16),
+            pltpu.VMEM((n_dp, 2, 2, 2, chunk, width), f32),
+            pltpu.VMEM((n_dp, 2, 2, chunk, width), bf16),
+            pltpu.VMEM((n_dp, 2, 2, chunk, width), bf16),
+            pltpu.VMEM((n_dp, 2, chunk, width), f32),
+            pltpu.VMEM((n_dp, 2, chunk, width), f32),
+            pltpu.VMEM((n_dp, 2, chunk, width), f32),
+            pltpu.VMEM((n_dp, 2, chunk, width), f32),
+            pltpu.VMEM((n_dp, 2, n_pipe, chunk, width), bf16),
+            pltpu.VMEM((n_dp, 2, n_pipe, chunk, width), bf16),
+            pltpu.VMEM((n_dp, 8, width), f32),
+            pltpu.VMEM((n_dp, 8, width), f32),
+            pltpu.VMEM((2, 8, width), f32),
+            pltpu.VMEM((2, 8, width), f32),
+            dma((4 + kv // (2 * width),)),
+            dma((2, 3)), dma((2, 3)), dma((2, 3)), dma((2, 3)),
+            dma((2, 4, 2)), dma((2, 4, 2)),
+            dma((n_dp,)), dma((n_dp,)),
+            dma((n_dp, 2, 2)), dma((n_dp, 2, 2)),
+            dma((n_dp, 2)), dma((n_dp, 2)),
+            dma((n_dp, 2)), dma((n_dp, 2)),
+            dma((2, 3)), dma((2, 3)),
+            dma((n_dp,)), dma((n_dp,)),
+            dma((2,)), dma((2,)),
+        ],
+        compiler_params=pltpu.CompilerParams(
+            collective_id=0, has_side_effects=True, vmem_limit_bytes=60 * 2**20
+        ),
+        cost_estimate=pl.CostEstimate(flops=flops, bytes_accessed=8 * 2**20, transcendentals=0),
+    )(
+        hidden.reshape(2, n_pipe, chunk, model),
+        gain.reshape(1, model),
+        w_value[0],
+        d_value[0].reshape(2, 2, 2 * chunk, kv),
+    )
+    return (hidden_grad.reshape(tokens, model), gain_grad.reshape(width), value_grad[None])
+
+
 def solution(mesh):
+    n_dp, n_pipe = mesh.shape["dp"], mesh.shape["pipe"]
+
+    def local(hidden, gain, w_value, d_value):
+        tokens, model = hidden.shape
+        width = w_value.shape[1]
+        cube = n_dp == 2 * 2 * 2 and n_pipe == 2 * 2
+        fits = tokens % (32 * n_pipe) == 0 and width % 128 == 0 and model == n_dp * width
+        fits = fits and d_value.shape[-1] % (4 * width) == 0 and n_dp * tokens <= model
+        if cube and fits:
+            return local_cube(n_dp, n_pipe, hidden, gain, w_value, d_value)
+        return local_general(hidden, gain, w_value, d_value)
+
     return jax.shard_map(
         local,
         mesh=mesh,

time: 280 us -> 84.2 us (0.30)
  waiting for transfers between devices: 213 us -> 0 us
  Pallas kernels: 0 us -> 77.6 us
  blocking collectives: 21.6 us -> 0 us
  matrix products: 15.4 us -> 0 us
  between operations: 14.5 us -> 0.66 us
  other arithmetic: 9.09 us -> 0 us
    reduce_scatter x2 -> x0, waiting for transfers between devices: 155 us -> none  [the longest x1 114 us: local(): lax.psum_scatter(weight_term(encoded, cotangent), 'dp', scatter_dimension...]
    pallas_call x0 -> x1, Pallas kernels: none -> 77.6 us  [local_cube(): pl.pallas_call(functools.partial(kernel, n_dp, n_pipe), out_shape=(jax.Sh...]
    all_gather x2 -> x0, waiting for transfers between devices: 57.6 us -> none  [the longest x1 57.6 us: local(): lax.all_gather(projection, 'dp', axis=0, tiled=True)]
    dot_general x2 -> x0, matrix products: 15.4 us -> none  [the longest x1 8.32 us: weight_term(): lax.dot_general(encoded, operand, (((0,), (0,)), ((), ())), preferred_ele...]
    unnamed x1 -> x0, blocking collectives: 11.5 us -> none
    psum x1 -> x0, blocking collectives: 10.1 us -> none  [local(): gain_share = lax.psum(gain_share, 'pipe')]
    broadcast_in_dim x1 -> x0, other arithmetic: 3.14 us -> none  [local(): return (grad_hidden, grad_gain, value_grad[None])]
  transfers between devices with their start and end apart: 4 -> 0, of which waited for: 3 -> 0; matrix products, arithmetic and copies ran while one was open for 4% -> 0% of each run, Pallas kernels for 0% -> 0%
where the time goes in v2:
time: 84.2 us; the launch traced here: 82.6 us
  Pallas kernels  77.6 us (92%)
  local copies, waits for them, and re-layouts  4.34 us (5%)
    pallas_call x1, Pallas kernels, local_cube(): pl.pallas_call(functools.partial(kernel, n_dp, n_pipe), out_shape=(jax.Sh...  77.6 us
    unnamed x7, local copies, waits for them, and re-layouts  4.34 us

profile of v2, /device:TPU:2, one launch (start us, length us, event | category | flops | bytes accessed | tf_op | source)
XLA Modules:
  0.0 82.6 jit_solution(12710140870751006283)
XLA Ops:
  0.6 77.6 %shard_map.67 = (bf16[2,4,32,2048]{3,2,1,0:T(8,128)(2,1)}, f32[1,256]{1,0:T(1,128)}, f32[256,2048]{1,0:T(8,128)}) custom-call(bf16[2,4,32,2048]{3,2,1,0:T(8,128)(2,1)} %bitcast.10, f32[1,2048]{1,0:T(1,128)} %bitcast.13, bf16[256,2048]{1,0:T(8,128)(2,1)} %bitcast.11, bf16[2,2,64,2048]{3,2,1,0:T(8,128)(2,1)} %bitcast.12), custom_call_target="tpu_custom_call" | custom-call | flops 4294967296 | bytes 8388608 | tf_op jit(solution)/shard_map/pallas_call | solution.py:376
  78.3 0.0 copy-start.1
  78.3 0.0 copy-start
  78.3 2.5 %copy.10 = bf16[256,2048]{1,0:T(8,128)(2,1)} copy(bf16[256,2048]{1,0:T(8,128)(2,1)} %bitcast.8) | data formatting | bytes 2097152
  80.7 0.0 copy-done.1
  80.7 0.6 copy.11
  81.3 0.0 copy-done
  81.3 1.3 %copy.12 = f32[1,256,2048]{2,1,0:T(8,128)} copy(f32[1,256,2048]{2,1,0:T(8,128)S(1)} %bitcast.7) | data formatting | bytes 4194304
Async XLA Ops:
  78.3 2.5 %copy-start.1 = (f32[1,256]{1,0:T(1,128)S(1)}, f32[1,256]{1,0:T(1,128)}, u32[]{:S(2)}) copy-start(f32[1,256]{1,0:T(1,128)} %get-tuple-element.7) | copy-start | bytes 3076
  78.3 3.0 %copy-start = (f32[256,2048]{1,0:T(8,128)S(1)}, f32[256,2048]{1,0:T(8,128)}, u32[]{:S(2)}) copy-start(f32[256,2048]{1,0:T(8,128)} %get-tuple-element.8) | copy-start | bytes 6291460
